TPU v7x, 32 devices: a whole 2x2x4 slice. The times are simulated.
32 devices in a mesh: groups: 2 (over y), grid: 4 (over z), band: 2 (over x), sub: 2 (over core).
Axes of the slice: x: 2, y: 2, z: 4, core: 2. Of those that a mesh axis runs over, the one named last changes fastest.
Arguments:
- filter_block: float32 [4, 32, 16, 8, 128], P(('groups', 'band'), 'grid', 'sub'), parts along dimension 0, may hold values from -300 to 300
- band_blocks: float32 [4, 2, 32, 16, 8, 128], P(('groups', 'band'), None, 'grid', 'sub'), parts along dimension 0, may hold values from -6 to 6
- potential: float32 [64, 16, 8], P(('groups', 'grid'), 'sub'), parts along dimension 0, may hold values from -1 to 4
- atom_plane: int32 [4096], P('groups'), parts along dimension 0, may hold values from 0 to 31
- block_slot: int32 [8], P('groups'), parts along dimension 0, may hold values from 0 to 3, each once
Outputs:
- correlation: float32 [4, 4, 128, 128], P(('groups', 'band')), parts along dimension 0
- energy: float32 [4, 4, 128, 128], P(('groups', 'band')), parts along dimension 0
There are 2 independent parts, one for each index of `groups`. A program takes and returns all parts, laid end to end along the dimension named above; each array names one. Nothing has to cross between parts.
All inputs are finite; a program needn't handle non-finite values.
Results may differ from a plain program's by a relative error of at most 0.0001.
Values sent between devices are 32-bit elements; how exact they have to be, the bound alone decides.
A program may use at most 64 MiB of HBM per device.

v0:
```python
import math

import jax
import jax.numpy as jnp
from jax import lax
from jax.sharding import PartitionSpec as P

STENCIL = (-205.0 / 72.0, 8.0 / 5.0, -1.0 / 5.0, 8.0 / 315.0, -1.0 / 560.0)
LOWER_EDGE = 1.0
KINETIC_TOP = 10.0
EPSILON = 1e-06


def extended(cells, sides, width):
    for axis, dim in sides:
        count = lax.axis_size(axis)
        head = lax.slice_in_dim(cells, 0, width, axis=dim)
        tail = lax.slice_in_dim(cells, cells.shape[dim] - width, cells.shape[dim], axis=dim)
        cells = jnp.concatenate(
            [
                lax.ppermute(tail, axis, [(i, (i + 1) % count) for i in range(count)]),
                cells,
                lax.ppermute(head, axis, [((i + 1) % count, i) for i in range(count)]),
            ],
            axis=dim,
        )
    return cells


def from_behind(x, axis, by):
    peers = lax.axis_size(axis)
    return lax.ppermute(x, axis, [(i, (i + by) % peers) for i in range(peers)])


def kinetic(padded, offset, depth_z, depth_y):
    centre = padded[offset : offset + depth_z, offset : offset + depth_y]
    summed = 3.0 * STENCIL[0] * centre
    for shift_by in range(1, 5):
        beside_all = padded[
            offset + shift_by : offset + shift_by + depth_z, offset : offset + depth_y
        ]
        beside_all = (
            beside_all
            + padded[offset - shift_by : offset - shift_by + depth_z, offset : offset + depth_y]
        )
        beside_all = (
            beside_all
            + padded[offset : offset + depth_z, offset + shift_by : offset + shift_by + depth_y]
        )
        beside_all = (
            beside_all
            + padded[offset : offset + depth_z, offset - shift_by : offset - shift_by + depth_y]
        )
        beside_all = beside_all + jnp.roll(centre, shift_by, 2) + jnp.roll(centre, -shift_by, 2)
        summed = summed + STENCIL[shift_by] * beside_all
    return -0.5 * summed


def apply_hamiltonian(orbital, effective):
    padded = extended(orbital, (("grid", 0), ("sub", 1)), 4)
    return (
        kinetic(padded, 4, orbital.shape[0], orbital.shape[1]) + effective[:, :, :, None] * orbital
    )


def add_block(correlation_acc, energy_acc, stored, source, slot, both, block_slot, orbitals):
    target = block_slot[2 * source + slot]
    products = lax.dot_general(
        stored,
        both,
        (((0,), (0,)), ((), ())),
        precision=lax.Precision.HIGHEST,
        preferred_element_type=jnp.float32,
    )
    zero_index = jnp.int32(0)
    correlation_acc = lax.dynamic_update_slice(
        correlation_acc, products[None, :, :orbitals], (target, zero_index, zero_index)
    )
    energy_acc = lax.dynamic_update_slice(
        energy_acc, products[None, :, orbitals:], (target, zero_index, zero_index)
    )
    return (correlation_acc, energy_acc)


def shards(filter_block, band_blocks, potential, atom_plane, block_slot):
    depth_z, depth_y, width_x, orbitals = filter_block.shape[1:]
    cells_dev = depth_z * depth_y * width_x
    planes_all = depth_z * lax.axis_size("grid")
    cells_all = cells_dev * lax.axis_size("grid") * lax.axis_size("sub")
    band_count = lax.axis_size("band")
    band_index = lax.axis_index("band")
    planes = lax.axis_index("grid") * depth_z + jnp.arange(depth_z, dtype=jnp.int32)
    counts = jnp.sum((planes[:, None] == atom_plane[None, :]).astype(jnp.float32), axis=1)
    effective = potential + (counts * (planes_all / atom_plane.shape[0]))[:, None, None]
    highest = lax.pmax(jnp.max(effective), ("grid", "sub"))
    ceiling = KINETIC_TOP + highest
    centre = 0.5 * (ceiling + LOWER_EDGE)
    spread = 0.5 * (ceiling - LOWER_EDGE)
    orbital = filter_block[0]
    section_one = (apply_hamiltonian(orbital, effective) - centre * orbital) / spread
    section_two = (
        2.0 * (apply_hamiltonian(section_one, effective) - centre * section_one) / spread - orbital
    )
    applied = apply_hamiltonian(section_two, effective)
    flat_two = section_two.reshape(cells_dev, orbitals)
    flat_applied = applied.reshape(cells_dev, orbitals)
    squares_dev = jnp.sum(section_two * section_two, axis=(0, 1, 2))
    squares_all = lax.psum(squares_dev, ("grid", "sub"))
    column_scale = lax.rsqrt(squares_all / cells_all + EPSILON)
    flat_two = flat_two * column_scale[None, :]
    flat_applied = flat_applied * column_scale[None, :]
    both = jnp.concatenate((flat_two, flat_applied), axis=1)
    visiting = band_blocks[0].reshape(2, cells_dev, orbitals)
    correlation_acc = jnp.zeros((2 * band_count, orbitals, orbitals), jnp.float32)
    energy_acc = jnp.zeros((2 * band_count, orbitals, orbitals), jnp.float32)
    for step in range(band_count):
        if step > 0:
            visiting = from_behind(visiting, "band", 1)
        source = (band_index - step) % band_count
        correlation_acc, energy_acc = add_block(
            correlation_acc, energy_acc, visiting[0], source, 0, both, block_slot, orbitals
        )
        correlation_acc, energy_acc = add_block(
            correlation_acc, energy_acc, visiting[1], source, 1, both, block_slot, orbitals
        )
    norm_factor = 1.0 / math.sqrt(cells_all)
    correlation, energy = lax.psum((correlation_acc, energy_acc), ("grid", "sub"))
    correlation = correlation * norm_factor
    energy = energy * norm_factor
    return (correlation[None], energy[None])


def solution(mesh):
    return jax.shard_map(
        shards,
        mesh=mesh,
        in_specs=(
            P(("groups", "band"), "grid", "sub", None, None),
            P(("groups", "band"), None, "grid", "sub", None, None),
            P(("groups", "grid"), "sub", None),
            P("groups"),
            P("groups"),
        ),
        out_specs=(
            P(("groups", "band"), None, None, None),
            P(("groups", "band"), None, None, None),
        ),
        check_vma=False,
    )
```

profile of v0, /device:TPU:0, one launch (start us, length us, event | category | flops | bytes accessed | tf_op | source)
XLA Modules:
  0.0 154.1 jit_solution(12441174357193743900)
XLA Ops:
  7.2 1.0 slice_bitcast_fusion.5
  8.2 5.1 %collective-permute-start = (f32[4,8,8,128]{3,2,1,0:T(8,128)S(1)}, f32[4,8,8,128]{3,2,1,0:T(8,128)S(1)}, u32[]{:S(2)}, u32[]{:S(2)}) collective-permute-start(f32[4,8,8,128]{3,2,1,0:T(8,128)S(1)} %get-tuple-element.68), channel_id=1, source_target_pairs={{4,0},{8,4},{12,8},{0,12},{5,1},{9,5},{13,9},{1,13},{6,2},{10,6},{... | collective-permute-start | bytes 393224 | tf_op jit(solution)/shard_map/ppermute | solution.py:23
  13.3 1.5 collective-permute-start.12
  15.0 0.8 fusion.130
  15.8 0.7 fusion.132
  16.5 0.6 fusion.134
  17.1 0.7 copy-done.10
  17.8 0.2 convert_reduce_fusion
  18.0 2.1 %collective-permute-done.1 = f32[4,8,8,128]{3,2,1,0:T(8,128)S(1)} collective-permute-done((f32[4,8,8,128]{3,2,1,0:T(8,128)S(1)}, f32[4,8,8,128]{3,2,1,0:T(8,128)S(1)}, u32[]{:S(2)}, u32[]{:S(2)}) %collective-permute-start.1) | collective-permute-done | bytes 131104 | tf_op jit(solution)/shard_map/ppermute | solution.py:21
  20.2 0.8 fusion.111
  21.0 0.5 collective-permute-start.3
  21.5 0.6 fusion.107
  22.2 15.6 %pmax.7 = f32[]{:T(128)} all-reduce(f32[]{:T(128)} %get-tuple-element.6), channel_id=1, replica_groups=mesh['groups'=2,'grid'=4,'band'=2,'sub'=2] {'grid','sub'}, use_global_device_ids=true, to_apply=%region_2.0 | all-reduce | flops 1 | bytes 8 | tf_op jit(solution)/shard_map/pmax | solution.py:95
  37.8 0.7 copy-done.9
  38.4 0.7 fusion.135
  47.9 1.1 fusion.108
  49.0 1.3 pad_maximum_fusion
  50.4 0.7 copy-done.7
  51.1 0.7 fusion.5
  52.1 2.0 %collective-permute-start.5 = (f32[4,8,8,128]{3,2,1,0:T(8,128)S(1)}, f32[4,8,8,128]{3,2,1,0:T(8,128)S(1)}, u32[]{:S(2)}, u32[]{:S(2)}) collective-permute-start(f32[4,8,8,128]{3,2,1,0:T(8,128)S(1)} %get-tuple-element.50), channel_id=1, source_target_pairs={{0,4},{4,8},{8,12},{12,0},{1,5},{5,9},{9,13},{13,1},{2,6},{6,10},{... | collective-permute-start | bytes 393224 | tf_op jit(solution)/shard_map/ppermute | solution.py:21
  54.1 5.7 %collective-permute-done.4 = f32[4,8,8,128]{3,2,1,0:T(8,128)S(1)} collective-permute-done((f32[4,8,8,128]{3,2,1,0:T(8,128)S(1)}, f32[4,8,8,128]{3,2,1,0:T(8,128)S(1)}, u32[]{:S(2)}, u32[]{:S(2)}) %collective-permute-start.4) | collective-permute-done | bytes 131104 | tf_op jit(solution)/shard_map/ppermute | solution.py:23
  60.0 0.5 collective-permute-start.7
  60.6 0.9 collective-permute-done.6
  61.5 0.4 collective-permute-done.7
  61.9 0.2 pad_maximum_fusion.1
  62.1 0.7 multiply_reduce_fusion
  62.8 0.7 fusion.119
  63.7 0.5 collective-permute-start.8
  64.2 1.6 %collective-permute-start.9 = (f32[4,8,8,128]{3,2,1,0:T(8,128)S(1)}, f32[4,8,8,128]{3,2,1,0:T(8,128)S(1)}, u32[]{:S(2)}, u32[]{:S(2)}) collective-permute-start(f32[4,8,8,128]{3,2,1,0:T(8,128)S(1)} %get-tuple-element.37), channel_id=1, source_target_pairs={{0,4},{4,8},{8,12},{12,0},{1,5},{5,9},{9,13},{13,1},{2,6},{6,10},{... | collective-permute-start | bytes 393224 | tf_op jit(solution)/shard_map/ppermute | solution.py:21
  65.8 15.8 %psum.21 = f32[128]{0:T(128)S(1)} all-reduce(f32[128]{0:T(128)S(1)} %get-tuple-element.4), channel_id=1, replica_groups=mesh['groups'=2,'grid'=4,'band'=2,'sub'=2] {'grid','sub'}, use_global_device_ids=true, to_apply=%region_4.5 | all-reduce | flops 128 | bytes 1024 | tf_op jit(solution)/shard_map/psum | solution.py:108
  81.8 0.5 collective-permute-start.11
  82.4 1.0 collective-permute-done.10
  83.3 0.4 collective-permute-done.11
  83.7 0.2 pad_maximum_fusion.2
  83.9 0.6 fusion.17
  84.6 1.0 convolution_bitcast_fusion.1
  85.7 1.0 convolution_bitcast_fusion.3
  86.7 0.1 copy.15
  86.8 1.0 convolution_bitcast_fusion.2
  87.8 0.1 copy.16
  88.0 0.1 copy.19
  88.1 1.0 convolution_bitcast_fusion
  89.3 0.1 copy.18
  89.4 0.1 copy.17
  89.7 0.7 copy-done.1
  90.5 54.4 %all-reduce.3.cloned.1.call-done = (f32[4,128,128]{2,1,0:T(8,128)}, f32[4,128,128]{2,1,0:T(8,128)}) async-done(((f32[4,128,128]{2,1,0:T(8,128)}, f32[4,128,128]{2,1,0:T(8,128)}), (f32[4,128,128]{2,1,0:T(8,128)}, f32[4,128,128]{2,1,0:T(8,128)})) %all-reduce.3.cloned.1.call-update) | async-done | bytes 524304 | tf_op jit(solution)/shard_map/psum | solution.py:127
  144.8 1.7 %multiply_bitcast_fusion = f32[1,4,128,128]{3,2,1,0:T(8,128)} fusion(f32[4,128,128]{2,1,0:T(8,128)} %get-tuple-element.3), kind=kLoop, calls=%fused_computation.171 | loop fusion | flops 65536 | bytes 524288 | tf_op jit(solution)/shard_map/broadcast_in_dim | solution.py:130
  146.5 0.7 multiply_bitcast_fusion.1
  (76 shorter events, 1.9 us)
Async XLA Ops:
  7.2 7.7 %copy-start = (f32[1,8,8,8,128]{4,3,2,1,0:T(8,128)S(1)}, f32[1,8,8,8,128]{4,3,2,1,0:T(8,128)}, u32[]{:S(2)}) copy-start(f32[1,8,8,8,128]{4,3,2,1,0:T(8,128)} %param.5) | copy-start | bytes 786436
  7.2 137.6 %all-reduce.3.cloned.1.call-start = ((), (), s32[]{:S(2)}) async-start(), calls=%async_computation | async-start | bytes 1048576 | tf_op jit(solution)/shard_map/psum | solution.py:127
  8.2 9.8 %collective-permute-start = (f32[4,8,8,128]{3,2,1,0:T(8,128)S(1)}, f32[4,8,8,128]{3,2,1,0:T(8,128)S(1)}, u32[]{:S(2)}, u32[]{:S(2)}) collective-permute-start(f32[4,8,8,128]{3,2,1,0:T(8,128)S(1)} %get-tuple-element.68), channel_id=1, source_target_pairs={{4,0},{8,4},{12,8},{0,12},{5,1},{9,5},{13,9},{1,13},{6,2},{10,6},{... | collective-permute-start | bytes 393224 | tf_op jit(solution)/shard_map/ppermute | solution.py:23
  13.3 6.8 %collective-permute-start.1 = (f32[4,8,8,128]{3,2,1,0:T(8,128)S(1)}, f32[4,8,8,128]{3,2,1,0:T(8,128)S(1)}, u32[]{:S(2)}, u32[]{:S(2)}) collective-permute-start(f32[4,8,8,128]{3,2,1,0:T(8,128)S(1)} %get-tuple-element.69), channel_id=1, source_target_pairs={{0,4},{4,8},{8,12},{12,0},{1,5},{5,9},{9,13},{13,1},{2,6},{6,10},{... | collective-permute-start | bytes 393224 | tf_op jit(solution)/shard_map/ppermute | solution.py:21
  13.3 71.2 %collective-permute-start.12 = (f32[2,512,128]{2,1,0:T(8,128)}, f32[2,512,128]{2,1,0:T(8,128)S(1)}, u32[]{:S(2)}, u32[]{:S(2)}) collective-permute-start(f32[2,512,128]{2,1,0:T(8,128)} %bitcast.66), channel_id=1, source_target_pairs={{0,2},{2,0},{1,3},{3,1},{4,6},{6,4},{5,7},{7,5},{8,10},{10,8},{9,1... | collective-permute-start | bytes 1572872 | tf_op jit(solution)/shard_map/ppermute | solution.py:32
  17.1 0.7 copy-start.10
  20.1 1.4 copy-start.8
  21.0 28.0 %collective-permute-start.2 = (f32[16,4,8,128]{3,2,1,0:T(8,128)}, f32[16,4,8,128]{3,2,1,0:T(8,128)}, u32[]{:S(2)}, u32[]{:S(2)}) collective-permute-start(f32[16,4,8,128]{3,2,1,0:T(8,128)} %get-tuple-element.20), channel_id=1, source_target_pairs={{1,0},{0,1},{3,2},{2,3},{5,4},{4,5},{7,6},{6,7},{9,8},{8,9},{11,10... | collective-permute-start | bytes 786440 | tf_op jit(solution)/shard_map/ppermute | solution.py:23
  21.0 28.0 %collective-permute-start.3 = (f32[16,4,8,128]{3,2,1,0:T(8,128)}, f32[16,4,8,128]{3,2,1,0:T(8,128)}, u32[]{:S(2)}, u32[]{:S(2)}) collective-permute-start(f32[16,4,8,128]{3,2,1,0:T(8,128)} %get-tuple-element.21), channel_id=1, source_target_pairs={{0,1},{1,0},{2,3},{3,2},{4,5},{5,4},{6,7},{7,6},{8,9},{9,8},{10,11... | collective-permute-start | bytes 786440 | tf_op jit(solution)/shard_map/ppermute | solution.py:21
  37.8 0.7 copy-start.9
  49.0 1.4 copy-start.3
  49.0 1.4 copy-start.4
  49.0 1.4 copy-start.5
  50.3 0.8 copy-start.7
  52.0 7.8 %collective-permute-start.4 = (f32[4,8,8,128]{3,2,1,0:T(8,128)S(1)}, f32[4,8,8,128]{3,2,1,0:T(8,128)S(1)}, u32[]{:S(2)}, u32[]{:S(2)}) collective-permute-start(f32[4,8,8,128]{3,2,1,0:T(8,128)S(1)} %get-tuple-element.51), channel_id=1, source_target_pairs={{4,0},{8,4},{12,8},{0,12},{5,1},{9,5},{13,9},{1,13},{6,2},{10,6},{... | collective-permute-start | bytes 393224 | tf_op jit(solution)/shard_map/ppermute | solution.py:23
  52.1 7.8 %collective-permute-start.5 = (f32[4,8,8,128]{3,2,1,0:T(8,128)S(1)}, f32[4,8,8,128]{3,2,1,0:T(8,128)S(1)}, u32[]{:S(2)}, u32[]{:S(2)}) collective-permute-start(f32[4,8,8,128]{3,2,1,0:T(8,128)S(1)} %get-tuple-element.50), channel_id=1, source_target_pairs={{0,4},{4,8},{8,12},{12,0},{1,5},{5,9},{9,13},{13,1},{2,6},{6,10},{... | collective-permute-start | bytes 393224 | tf_op jit(solution)/shard_map/ppermute | solution.py:21
  59.9 1.6 %collective-permute-start.6 = (f32[16,4,8,128]{3,2,1,0:T(8,128)S(1)}, f32[16,4,8,128]{3,2,1,0:T(8,128)S(1)}, u32[]{:S(2)}, u32[]{:S(2)}) collective-permute-start(f32[16,4,8,128]{3,2,1,0:T(8,128)S(1)} %get-tuple-element.16), channel_id=1, source_target_pairs={{1,0},{0,1},{3,2},{2,3},{5,4},{4,5},{7,6},{6,7},{9,8},{8,9},{11,10... | collective-permute-start | bytes 786440 | tf_op jit(solution)/shard_map/ppermute | solution.py:23
  60.0 1.9 %collective-permute-start.7 = (f32[16,4,8,128]{3,2,1,0:T(8,128)S(1)}, f32[16,4,8,128]{3,2,1,0:T(8,128)S(1)}, u32[]{:S(2)}, u32[]{:S(2)}) collective-permute-start(f32[16,4,8,128]{3,2,1,0:T(8,128)S(1)} %get-tuple-element.17), channel_id=1, source_target_pairs={{0,1},{1,0},{2,3},{3,2},{4,5},{5,4},{6,7},{7,6},{8,9},{9,8},{10,11... | collective-permute-start | bytes 786440 | tf_op jit(solution)/shard_map/ppermute | solution.py:21
  63.7 17.9 %collective-permute-start.8 = (f32[4,8,8,128]{3,2,1,0:T(8,128)}, f32[4,8,8,128]{3,2,1,0:T(8,128)S(1)}, u32[]{:S(2)}, u32[]{:S(2)}) collective-permute-start(f32[4,8,8,128]{3,2,1,0:T(8,128)} %get-tuple-element.36), channel_id=1, source_target_pairs={{4,0},{8,4},{12,8},{0,12},{5,1},{9,5},{13,9},{1,13},{6,2},{10,6},{... | collective-permute-start | bytes 393224 | tf_op jit(solution)/shard_map/ppermute | solution.py:23
  64.2 17.4 %collective-permute-start.9 = (f32[4,8,8,128]{3,2,1,0:T(8,128)S(1)}, f32[4,8,8,128]{3,2,1,0:T(8,128)S(1)}, u32[]{:S(2)}, u32[]{:S(2)}) collective-permute-start(f32[4,8,8,128]{3,2,1,0:T(8,128)S(1)} %get-tuple-element.37), channel_id=1, source_target_pairs={{0,4},{4,8},{8,12},{12,0},{1,5},{5,9},{9,13},{13,1},{2,6},{6,10},{... | collective-permute-start | bytes 393224 | tf_op jit(solution)/shard_map/ppermute | solution.py:21
  81.7 1.6 %collective-permute-start.10 = (f32[16,4,8,128]{3,2,1,0:T(8,128)S(1)}, f32[16,4,8,128]{3,2,1,0:T(8,128)S(1)}, u32[]{:S(2)}, u32[]{:S(2)}) collective-permute-start(f32[16,4,8,128]{3,2,1,0:T(8,128)S(1)} %get-tuple-element.12), channel_id=1, source_target_pairs={{1,0},{0,1},{3,2},{2,3},{5,4},{4,5},{7,6},{6,7},{9,8},{8,9},{11,10... | collective-permute-start | bytes 786440 | tf_op jit(solution)/shard_map/ppermute | solution.py:23
  81.8 1.9 %collective-permute-start.11 = (f32[16,4,8,128]{3,2,1,0:T(8,128)S(1)}, f32[16,4,8,128]{3,2,1,0:T(8,128)S(1)}, u32[]{:S(2)}, u32[]{:S(2)}) collective-permute-start(f32[16,4,8,128]{3,2,1,0:T(8,128)S(1)} %get-tuple-element.13), channel_id=1, source_target_pairs={{0,1},{1,0},{2,3},{3,2},{4,5},{5,4},{6,7},{7,6},{8,9},{9,8},{10,11... | collective-permute-start | bytes 786440 | tf_op jit(solution)/shard_map/ppermute | solution.py:21
  89.6 0.7 copy-start.1
  89.7 0.8 copy-start.2
  144.8 1.7 %copy-start.6 = (f32[4,128,128]{2,1,0:T(8,128)S(1)}, f32[4,128,128]{2,1,0:T(8,128)}, u32[]{:S(2)}) copy-start(f32[4,128,128]{2,1,0:T(8,128)} %get-tuple-element.2) | copy-start | bytes 786436
Sparse Core Ops, SparseCore 0:
  90.6 54.1 all-reduce.2
where the time goes:
time: 155 us; the launch traced here: 154 us
  waiting for transfers between devices  64.8 us (42%)
  blocking collectives  31.4 us (20%)
  between operations  23.4 us (15%)
  starting transfers between devices  12.4 us (8%)
  local copies, waits for them, and re-layouts  11 us (7%)
  other arithmetic  7.13 us (5%)
  matrix products  3.98 us (3%)
    psum x1, waiting for transfers between devices, shards(): lax.psum((correlation_acc, energy_acc), ('grid', 'sub'))  54.4 us
    psum x1, blocking collectives, shards(): squares_all = lax.psum(squares_dev, ('grid', 'sub'))  15.8 us
    pmax x1, blocking collectives, shards(): highest = lax.pmax(jnp.max(effective), ('grid', 'sub'))  15.6 us
    ppermute x6, waiting for transfers between devices, extended(): lax.ppermute(head, axis, [((i + 1) % count, i) for i in range(count)])  7.61 us
    ppermute x6, starting transfers between devices, extended(): lax.ppermute(head, axis, [((i + 1) % count, i) for i in range(count)])  5.77 us
    ppermute x6, starting transfers between devices, extended(): lax.ppermute(tail, axis, [(i, (i + 1) % count) for i in range(count)])  5.13 us
    dot_general x4, matrix products, add_block(): lax.dot_general(stored, both, (((0,), (0,)), ((), ())), precision=lax.Pre...  3.98 us
  transfers between devices with their start and end apart: 14, of which 7 were waited for; matrix products, arithmetic and copies ran while one was open for 7% of the time, Pallas kernels for 0%

commit v1 on v0

v1 whole, which is shorter than its diff:
```python
import functools
import math

import jax
import jax.numpy as jnp
from jax import lax
from jax.experimental import pallas as pl
from jax.experimental.pallas import tpu as pltpu
from jax.sharding import PartitionSpec as P

STENCIL = (-205.0 / 72.0, 8.0 / 5.0, -1.0 / 5.0, 8.0 / 315.0, -1.0 / 560.0)
LOWER_EDGE = 1.0
KINETIC_TOP = 10.0
EPSILON = 1e-06
HALO = 4
CHUNKS = 4
MESH = pl.DeviceIdType.MESH


def remote(src, dst, send_sem, recv_sem, **device):
    return pltpu.make_async_remote_copy(
        src_ref=src,
        dst_ref=dst,
        send_sem=send_sem,
        recv_sem=recv_sem,
        device_id=device,
        device_id_type=MESH,
    )


def split(value):
    high = value.astype(jnp.bfloat16)
    return high, (value - high.astype(jnp.float32)).astype(jnp.bfloat16)


def kernel(
    nz, nb, x_hbm, q_hbm, pot, atoms, out,
    f0, f1, f2, applied, acc, eff, ypeer, qbuf, qt_high, qt_low,
    consts, tops, squares, part_out, part_in, part_sum, from_low, from_high, to_high, to_low,
    load_sem, z_send, z_recv, y_send, y_recv, q_send, q_recv,
    top_send, top_recv, square_send, square_recv, part_send, part_recv,
    up_send, up_recv, down_send, down_recv, out_send, out_recv,
):
    g, s, b = lax.axis_index("grid"), lax.axis_index("sub"), lax.axis_index("band")
    other = 1 - s
    above, below = lax.rem(g + 1, nz), lax.rem(g + nz - 1, nz)
    depth_z, depth_y, width_x, orbitals = acc.shape
    ranks = 2 * nz
    me = 2 * g + s
    planes_all = nz * depth_z
    cells_dev = depth_z * depth_y * width_x
    cells_all = cells_dev * ranks
    half = nb * orbitals
    chunk = half // CHUNKS
    fields = (f0, f1, f2)
    lower_half = depth_z // 2

    loads = [pltpu.make_async_copy(x_hbm.at[0], f0.at[pl.ds(HALO, depth_z)], load_sem.at[0])]
    for slot in range(2):
        loads.append(
            pltpu.make_async_copy(q_hbm.at[0, slot], qbuf.at[2 * b + slot], load_sem.at[1 + slot])
        )
    for load in loads:
        load.start()

    barrier = pltpu.get_barrier_semaphore()

    def greet(step, carry):
        rank = lax.rem(me + step, ranks)
        pl.semaphore_signal(
            barrier, inc=1, device_id={"grid": rank // 2, "sub": lax.rem(rank, 2)}, device_id_type=MESH
        )
        return carry

    lax.fori_loop(1, ranks, greet, 0)
    for step in range(1, nb):
        pl.semaphore_signal(
            barrier, inc=1, device_id={"band": lax.rem(b + step, nb)}, device_id_type=MESH
        )
    pl.semaphore_wait(barrier, ranks - 1 + nb - 1)

    def z_copy(step, side):
        field = fields[step]
        if side == 0:
            src = pl.ds(HALO, HALO)
            dst = field.at[pl.ds(HALO + depth_z, HALO)]
            where = below
        else:
            src = pl.ds(depth_z, HALO)
            dst = field.at[pl.ds(0, HALO)]
            where = above
        source = field.at[src]
        if step == 0:
            source = x_hbm.at[0, pl.ds(0 if side == 0 else depth_z - HALO, HALO)]
        return remote(source, dst, z_send.at[step, side], z_recv.at[step, 1 - side], grid=where)

    def y_copy(step, side):
        planes = pl.ds(side * lower_half, lower_half)
        source = fields[step].at[pl.ds(HALO + side * lower_half, lower_half)]
        if step == 0:
            source = x_hbm.at[0, planes]
        return remote(
            source, ypeer.at[step, planes], y_send.at[step, side], y_recv.at[step, side], sub=other
        )

    def q_copy(step, slot):
        return remote(
            q_hbm.at[0, slot], qbuf.at[2 * b + slot],
            q_send.at[step - 1, slot], q_recv.at[step - 1, slot], band=lax.rem(b + step, nb),
        )

    for side in range(2):
        z_copy(0, side).start()
    for side in range(2):
        y_copy(0, side).start()
    for step in range(1, nb):
        for slot in range(2):
            q_copy(step, slot).start()

    centre_term = -0.5 * 3.0 * STENCIL[0]
    eye = lax.broadcasted_iota(jnp.int32, (width_x, width_x), 0) == lax.broadcasted_iota(
        jnp.int32, (width_x, width_x), 1
    )
    atom_total = atoms.shape[0] * atoms.shape[1]

    def plane_potential(p, top):
        hits = jnp.where(atoms[...] == g * depth_z + p, 1.0, 0.0)
        count = jnp.sum(jnp.sum(hits, axis=0, keepdims=True), axis=1, keepdims=True)
        offset = count * (planes_all / atom_total)
        for y in range(depth_y):
            row = jnp.broadcast_to(pot[p, pl.ds(y, 1), :], (width_x, width_x))
            column = jnp.sum(jnp.where(eye, row, 0.0), axis=1, keepdims=True)
            cell = jnp.broadcast_to(column + offset, (width_x, orbitals))
            top = jnp.maximum(top, cell)
            eff[p, y] = cell + centre_term
        return top

    tops[me] = lax.fori_loop(
        0, depth_z, plane_potential, jnp.full((width_x, orbitals), -jnp.inf, jnp.float32)
    )

    def rank_copy(buffer, send_sem, recv_sem, step):
        rank = lax.rem(me + step, ranks)
        return remote(
            buffer.at[me], buffer.at[me], send_sem.at[step], recv_sem.at[step],
            grid=rank // 2, sub=lax.rem(rank, 2),
        )

    def send_ranks(buffer, send_sem, recv_sem):
        def one(step, carry):
            rank_copy(buffer, send_sem, recv_sem, step).start()
            return carry

        lax.fori_loop(1, ranks, one, 0)

    def wait_ranks(buffer, send_sem, recv_sem):
        def one(step, carry):
            rank_copy(buffer, send_sem, recv_sem, step).wait_recv()
            return carry

        lax.fori_loop(1, ranks, one, 0)

    send_ranks(tops, top_send, top_recv)

    def pre(step):
        field = fields[step]
        for side in range(2):
            y_copy(step, side).wait_recv()

        def one(p, carry):
            own = field[HALO + p]
            peer = ypeer[step, p]
            row = jnp.concatenate((peer[depth_y - HALO :], own, peer[:HALO]), axis=0)
            total = eff[p] * own
            for k in range(1, 5):
                near = row[HALO + k : HALO + k + depth_y] + row[HALO - k : HALO - k + depth_y]
                near = near + pltpu.roll(own, k % width_x, 1) + pltpu.roll(own, (-k) % width_x, 1)
                total = total + (-0.5 * STENCIL[k]) * near
            acc[p] = total
            return carry

        lax.fori_loop(0, depth_z, one, 0)

    def finish(step, side):
        field = fields[step]
        z_copy(step, 1 - side).wait_recv()

        def one(p, carry):
            total = acc[p]
            for k in range(1, 5):
                total = total + (-0.5 * STENCIL[k]) * (field[HALO + p + k] + field[HALO + p - k])
            if step == 2:
                applied[p] = total
            else:
                shifted = (total - consts[0][None] * field[HALO + p]) * consts[1][None]
                if step == 0:
                    f1[HALO + p] = shifted
                else:
                    f2[HALO + p] = 2.0 * shifted - f0[HALO + p]
            return carry

        lax.fori_loop(side * lower_half, (side + 1) * lower_half, one, 0)
        if step < 2:
            z_copy(step + 1, side).start()
            y_copy(step + 1, side).start()

    def finish_both(step):
        @pl.when(g == 0)
        def _():
            finish(step, 1)
            finish(step, 0)

        @pl.when(g != 0)
        def _():
            finish(step, 0)
            finish(step, 1)

    def transposed(k):
        flat = qbuf[k].reshape(cells_dev, orbitals)
        high, low = split(flat.T)
        rows = pl.ds(pl.multiple_of(k * orbitals, orbitals), orbitals)
        qt_high[rows] = high
        qt_low[rows] = low

    loads[0].wait()
    pre(0)
    wait_ranks(tops, top_send, top_recv)
    highest = jnp.max(jnp.max(tops[...], axis=0), axis=0, keepdims=True)
    ceiling = KINETIC_TOP + jnp.broadcast_to(highest, (8, orbitals))
    consts[0] = 0.5 * (ceiling + LOWER_EDGE)
    consts[1] = 1.0 / (0.5 * (ceiling - LOWER_EDGE))
    finish_both(0)
    pre(1)
    for slot in range(2):
        loads[1 + slot].wait()
        transposed(2 * b + slot)
    finish_both(1)

    def square(p, total):
        plane = f2[HALO + p]
        return total + jnp.sum(plane * plane, axis=0)

    squares[me] = lax.fori_loop(0, depth_z, square, jnp.zeros((width_x, orbitals), jnp.float32))
    send_ranks(squares, square_send, square_recv)

    for step in range(1, nb):
        source = lax.rem(b + nb - step, nb)
        for slot in range(2):
            q_copy(step, slot).wait_recv()
            transposed(2 * source + slot)

    def product(rows, high, low):
        dot = functools.partial(jnp.dot, preferred_element_type=jnp.float32)
        first = qt_high[rows]
        return dot(first, high) + (dot(first, low) + dot(qt_low[rows], high))

    def part_copy(phase):
        return remote(
            part_out.at[phase], part_in.at[phase], part_send.at[phase], part_recv.at[phase], sub=other
        )

    mine = pl.ds(pl.multiple_of(s * half, half), half)
    theirs = pl.ds(pl.multiple_of(other * half, half), half)

    def start_gram(phase, field):
        high, low = split(field.reshape(cells_dev, orbitals))
        part_out[phase] = product(theirs, high, low)
        part_copy(phase).start()
        part_sum[phase] = product(mine, high, low)

    def chunk_rows(c):
        return pl.ds(c * chunk, chunk)

    def up_copy(phase, c, first):
        source = part_sum if first else to_high
        return remote(
            source.at[phase, chunk_rows(c)], from_low.at[phase, chunk_rows(c)],
            up_send.at[phase, c], up_recv.at[phase, c], grid=above,
        )

    def down_copy(phase, c, first):
        source = part_sum if first else to_low
        return remote(
            source.at[phase, chunk_rows(c)], from_high.at[phase, chunk_rows(c)],
            down_send.at[phase, c], down_recv.at[phase, c], grid=below,
        )

    def reduce_sub(phase):
        part_copy(phase).wait_recv()
        part_sum[phase] = part_sum[phase] + part_in[phase]

        @pl.when(g == 0)
        def _():
            for c in range(CHUNKS):
                up_copy(phase, c, True).start()

        @pl.when(g == nz - 1)
        def _():
            for c in range(CHUNKS):
                down_copy(phase, c, True).start()

    def relay_up(phase):
        @pl.when(jnp.logical_and(g > 0, g < nz - 1))
        def _():
            for c in range(CHUNKS):
                up_copy(phase, c, False).wait_recv()
                to_high[phase, chunk_rows(c)] = (
                    from_low[phase, chunk_rows(c)] + part_sum[phase, chunk_rows(c)]
                )
                up_copy(phase, c, False).start()

    def relay_down(phase):
        @pl.when(jnp.logical_and(g > 0, g < nz - 1))
        def _():
            for c in range(CHUNKS):
                down_copy(phase, c, False).wait_recv()
                to_low[phase, chunk_rows(c)] = (
                    from_high[phase, chunk_rows(c)] + part_sum[phase, chunk_rows(c)]
                )
                down_copy(phase, c, False).start()

    def relay(phase):
        @pl.when(g < nz // 2)
        def _():
            relay_up(phase)
            relay_down(phase)

        @pl.when(g >= nz // 2)
        def _():
            relay_down(phase)
            relay_up(phase)

    def out_copy(phase, c):
        rows = pl.ds(pl.multiple_of(s * half + c * chunk, chunk), chunk)
        return remote(
            out.at[phase, rows], out.at[phase, rows],
            out_send.at[phase, c], out_recv.at[phase, c], sub=other,
        )

    def conclude(phase, factor):
        for c in range(CHUNKS):
            rows = pl.ds(pl.multiple_of(s * half + c * chunk, chunk), chunk)
            own = part_sum[phase, chunk_rows(c)]

            @pl.when(g == 0)
            def _():
                down_copy(phase, c, False).wait_recv()
                out[phase, rows] = (own + from_high[phase, chunk_rows(c)]) * factor

            @pl.when(g == nz - 1)
            def _():
                up_copy(phase, c, False).wait_recv()
                out[phase, rows] = (own + from_low[phase, chunk_rows(c)]) * factor

            @pl.when(jnp.logical_and(g > 0, g < nz - 1))
            def _():
                out[phase, rows] = (
                    to_high[phase, chunk_rows(c)] + from_high[phase, chunk_rows(c)]
                ) * factor

            out_copy(phase, c).start()

    start_gram(0, f2[pl.ds(HALO, depth_z)])
    pre(2)
    reduce_sub(0)
    finish_both(2)
    start_gram(1, applied[...])
    relay(0)
    reduce_sub(1)
    wait_ranks(squares, square_send, square_recv)
    total = jnp.sum(jnp.sum(squares[...], axis=0), axis=0, keepdims=True)
    factor = lax.rsqrt(total / cells_all + EPSILON) * (1.0 / math.sqrt(cells_all))
    conclude(0, factor)
    relay(1)
    conclude(1, factor)

    for phase in range(2):
        for c in range(CHUNKS):
            out_copy(phase, c).wait()
    for step in range(3):
        for side in range(2):
            z_copy(step, side).wait_send()
            y_copy(step, side).wait_send()
    for step in range(1, nb):
        for slot in range(2):
            q_copy(step, slot).wait_send()

    def drain(step, carry):
        rank_copy(tops, top_send, top_recv, step).wait_send()
        rank_copy(squares, square_send, square_recv, step).wait_send()
        return carry

    lax.fori_loop(1, ranks, drain, 0)
    for phase in range(2):
        part_copy(phase).wait_send()

        @pl.when(g < nz - 1)
        def _():
            for c in range(CHUNKS):
                up_copy(phase, c, False).wait_send()

        @pl.when(g > 0)
        def _():
            for c in range(CHUNKS):
                down_copy(phase, c, False).wait_send()


def shards(nz, nb, filter_block, band_blocks, potential, atom_plane, block_slot):
    cells = filter_block.shape[1:]
    depth_z, depth_y, width_x, orbitals = cells
    ranks = 2 * nz
    stored = 2 * nb
    half = nb * orbitals
    cells_dev = depth_z * depth_y * width_x
    f32 = jnp.float32
    padded = pltpu.VMEM((depth_z + 2 * HALO,) + cells[1:], f32)
    whole = pltpu.VMEM(cells, f32)
    gram = pltpu.VMEM((2, half, orbitals), f32)
    dma = pltpu.SemaphoreType.DMA
    products = pl.pallas_call(
        functools.partial(kernel, nz, nb),
        out_shape=jax.ShapeDtypeStruct((2, stored * orbitals, orbitals), f32),
        in_specs=[
            pl.BlockSpec(memory_space=pl.ANY),
            pl.BlockSpec(memory_space=pl.ANY),
            pl.BlockSpec(memory_space=pltpu.VMEM),
            pl.BlockSpec(memory_space=pltpu.VMEM),
        ],
        out_specs=pl.BlockSpec(memory_space=pltpu.VMEM),
        scratch_shapes=[
            padded, padded, padded, whole, whole, whole,
            pltpu.VMEM((3,) + cells, f32),
            pltpu.VMEM((stored,) + cells, f32),
            pltpu.VMEM((stored * orbitals, cells_dev), jnp.bfloat16),
            pltpu.VMEM((stored * orbitals, cells_dev), jnp.bfloat16),
            pltpu.VMEM((2, 8, orbitals), f32),
            pltpu.VMEM((ranks, width_x, orbitals), f32),
            pltpu.VMEM((ranks, width_x, orbitals), f32),
            gram, gram, gram, gram, gram, gram, gram,
            dma((3,)),
            dma((3, 2)), dma((3, 2)), dma((3, 2)), dma((3, 2)),
            dma((nb, 2)), dma((nb, 2)),
            dma((ranks,)), dma((ranks,)), dma((ranks,)), dma((ranks,)),
            dma((2,)), dma((2,)),
            dma((2, CHUNKS)), dma((2, CHUNKS)), dma((2, CHUNKS)), dma((2, CHUNKS)),
            dma((2, CHUNKS)), dma((2, CHUNKS)),
        ],
        compiler_params=pltpu.CompilerParams(
            collective_id=0, has_side_effects=True, vmem_limit_bytes=48 * 1024 * 1024
        ),
        cost_estimate=pl.CostEstimate(
            flops=4 * cells_dev * orbitals * stored * orbitals,
            bytes_accessed=4 * orbitals * (3 * cells_dev + 2 * stored * orbitals),
            transcendentals=0,
        ),
    )(filter_block, band_blocks, potential, atom_plane.reshape(-1, 128))
    blocks = products.reshape(2, stored, orbitals, orbitals)
    placed = []
    for target in range(stored):
        block = jnp.zeros((2, orbitals, orbitals), f32)
        for k in range(stored):
            block = jnp.where(block_slot[k] == target, blocks[:, k], block)
        placed.append(block)
    placed = jnp.stack(placed, axis=1)
    return placed[0][None], placed[1][None]


def solution(mesh):
    return jax.shard_map(
        functools.partial(shards, mesh.shape["grid"], mesh.shape["band"]),
        mesh=mesh,
        in_specs=(
            P(("groups", "band"), "grid", "sub", None, None),
            P(("groups", "band"), None, "grid", "sub", None, None),
            P(("groups", "grid"), "sub", None),
            P("groups"),
            P("groups"),
        ),
        out_specs=(
            P(("groups", "band"), None, None, None),
            P(("groups", "band"), None, None, None),
        ),
        check_vma=False,
    )
```

time: 155 us -> 59 us (0.38)
  waiting for transfers between devices: 64.8 us -> 0 us
  Pallas kernels: 0 us -> 43.2 us
  blocking collectives: 31.4 us -> 0 us
  between operations: 23.4 us -> 10.9 us
  starting transfers between devices: 12.4 us -> 0 us
  other arithmetic: 7.13 us -> 0.12 us
  local copies, waits for them, and re-layouts: 11 us -> 4.29 us
  matrix products: 3.98 us -> 0 us
    psum x1 -> x0, waiting for transfers between devices: 54.4 us -> none  [shards(): lax.psum((correlation_acc, energy_acc), ('grid', 'sub'))]
    pallas_call x0 -> x1, Pallas kernels: none -> 43.2 us  [shards(): pl.pallas_call(functools.partial(kernel, nz, nb), out_shape=jax.ShapeDtyp...]
    psum x1 -> x0, blocking collectives: 15.8 us -> none  [shards(): squares_all = lax.psum(squares_dev, ('grid', 'sub'))]
    pmax x1 -> x0, blocking collectives: 15.6 us -> none  [shards(): highest = lax.pmax(jnp.max(effective), ('grid', 'sub'))]
    ppermute x13 -> x0, starting transfers between devices: 12.4 us -> none  [the longest x6 5.77 us: extended(): lax.ppermute(head, axis, [((i + 1) % count, i) for i in range(count)])]
    ppermute x13 -> x0, waiting for transfers between devices: 10.5 us -> none  [the longest x6 7.61 us: extended(): lax.ppermute(head, axis, [((i + 1) % count, i) for i in range(count)])]
    slice x28 -> x2, local copies, waits for them, and re-layouts: 6.51 us -> 2.29 us  [the longest x1 1.46 us: shards(): block = jnp.where(block_slot[k] == target, blocks[:, k], block)]
    dot_general x4 -> x0, matrix products: 3.98 us -> none  [add_block(): lax.dot_general(stored, both, (((0,), (0,)), ((), ())), precision=lax.Pre...]
  transfers between devices with their start and end apart: 14 -> 0, of which waited for: 7 -> 0; matrix products, arithmetic and copies ran while one was open for 7% -> 0% of each run, Pallas kernels for 0% -> 0%
where the time goes in v1:
time: 59 us; the launch traced here: 58.5 us
  Pallas kernels  43.2 us (73%)
  between operations  10.9 us (18%)
  local copies, waits for them, and re-layouts  4.29 us (7%)
    pallas_call x1, Pallas kernels, shards(): pl.pallas_call(functools.partial(kernel, nz, nb), out_shape=jax.ShapeDtyp...  43.2 us
    unnamed x8, local copies, waits for them, and re-layouts  2 us
    slice x1, local copies, waits for them, and re-layouts, shards(): block = jnp.where(block_slot[k] == target, blocks[:, k], block)  1.46 us

profile of v1, /device:TPU:0, one launch (start us, length us, event | category | flops | bytes accessed | tf_op | source)
XLA Modules:
  0.0 58.5 jit_solution(5186743427114627080)
XLA Ops:
  0.6 0.0 copy-start.2
  0.6 1.5 %fusion.1 = (s32[1]{0:T(128)}, s32[1]{0:T(128)}, s32[1]{0:T(128)}, s32[1]{0:T(128)}) fusion(s32[4]{0:T(128)} %param.9), kind=kLoop, calls=%fused_computation.6 | loop fusion | bytes 32 | tf_op jit(solution)/shard_map/slice | solution.py:462
  5.3 0.0 copy-start.3
  7.2 0.0 copy-done.2
  7.2 0.0 copy-done.3
  7.2 0.0 copy-start
  7.2 1.0 %copy-done = f32[1,2,8,8,8,128]{5,4,3,2,1,0:T(8,128)S(1)} copy-done((f32[1,2,8,8,8,128]{5,4,3,2,1,0:T(8,128)S(1)}, f32[1,2,8,8,8,128]{5,4,3,2,1,0:T(8,128)}, u32[]{:S(2)}) %copy-start) | copy-done | bytes 524312
  8.3 0.0 copy-start.1
  8.3 0.9 %copy-done.1 = f32[1,8,8,8,128]{4,3,2,1,0:T(8,128)S(1)} copy-done((f32[1,8,8,8,128]{4,3,2,1,0:T(8,128)S(1)}, f32[1,8,8,8,128]{4,3,2,1,0:T(8,128)}, u32[]{:S(2)}) %copy-start.1) | copy-done | bytes 262168
  9.2 43.2 %shard_map.68 = f32[2,512,128]{2,1,0:T(8,128)S(1)} custom-call(f32[1,8,8,8,128]{4,3,2,1,0:T(8,128)S(1)} %copy-done.1, f32[1,2,8,8,8,128]{5,4,3,2,1,0:T(8,128)S(1)} %copy-done, f32[8,8,8]{2,1,0:T(8,128)S(1)} %copy-done.2, s32[16,128]{1,0:T(8,128)S(1)} %bitcast.20), custom_call_target="tpu_custom_call" | custom-call | flops 134217728 | bytes 1310720 | tf_op jit(solution)/shard_map/pallas_call | solution.py:420
  57.7 0.8 %fusion = (f32[1,4,128,128]{3,2,1,0:T(8,128)}, f32[1,4,128,128]{3,2,1,0:T(8,128)}) fusion(f32[2,4,128,128]{3,2,1,0:T(8,128)S(1)} %pad_maximum_fusion), kind=kLoop, calls=%fused_computation.5 | loop fusion | bytes 1048576 | tf_op jit(solution)/shard_map/slice | solution.py:465
  (3 shorter events, 0.1 us)
Async XLA Ops:
  0.6 6.6 %copy-start.2 = (f32[8,8,8]{2,1,0:T(8,128)S(1)}, f32[8,8,8]{2,1,0:T(8,128)}, u32[]{:S(2)}) copy-start(f32[8,8,8]{2,1,0:T(8,128)} %pot.1) | copy-start | bytes 6148
  5.3 1.9 %copy-start.3 = (s32[2048]{0:T(1024)S(1)}, s32[2048]{0:T(1024)}, u32[]{:S(2)}) copy-start(s32[2048]{0:T(1024)} %param.8) | copy-start | bytes 24580
  7.2 1.0 %copy-start = (f32[1,2,8,8,8,128]{5,4,3,2,1,0:T(8,128)S(1)}, f32[1,2,8,8,8,128]{5,4,3,2,1,0:T(8,128)}, u32[]{:S(2)}) copy-start(f32[1,2,8,8,8,128]{5,4,3,2,1,0:T(8,128)} %q_hbm.1) | copy-start | bytes 1572868
  8.3 0.9 %copy-start.1 = (f32[1,8,8,8,128]{4,3,2,1,0:T(8,128)S(1)}, f32[1,8,8,8,128]{4,3,2,1,0:T(8,128)}, u32[]{:S(2)}) copy-start(f32[1,8,8,8,128]{4,3,2,1,0:T(8,128)} %x_hbm.1) | copy-start | bytes 786436

commit v2 on v1

--- a/solution.py
+++ b/solution.py
@@ -34,8 +34,8 @@
 
 
 def kernel(
-    nz, nb, x_hbm, q_hbm, pot, atoms, out,
-    f0, f1, f2, applied, acc, eff, ypeer, qbuf, qt_high, qt_low,
+    nz, nb, slots, x_hbm, q_hbm, pot_hbm, atoms_hbm, corr, energy,
+    pot, atoms, f0, f1, f2, applied, acc, eff, ypeer, qbuf, qt_high, qt_low,
     consts, tops, squares, part_out, part_in, part_sum, from_low, from_high, to_high, to_low,
     load_sem, z_send, z_recv, y_send, y_recv, q_send, q_recv,
     top_send, top_recv, square_send, square_recv, part_send, part_recv,
@@ -60,6 +60,8 @@
         loads.append(
             pltpu.make_async_copy(q_hbm.at[0, slot], qbuf.at[2 * b + slot], load_sem.at[1 + slot])
         )
+    loads.append(pltpu.make_async_copy(pot_hbm, pot, load_sem.at[3]))
+    loads.append(pltpu.make_async_copy(atoms_hbm, atoms, load_sem.at[4]))
     for load in loads:
         load.start()
 
@@ -135,6 +137,8 @@
             eff[p, y] = cell + centre_term
         return top
 
+    loads[3].wait()
+    loads[4].wait()
     tops[me] = lax.fori_loop(
         0, depth_z, plane_potential, jnp.full((width_x, orbitals), -jnp.inf, jnp.float32)
     )
@@ -218,9 +222,8 @@
     def transposed(k):
         flat = qbuf[k].reshape(cells_dev, orbitals)
         high, low = split(flat.T)
-        rows = pl.ds(pl.multiple_of(k * orbitals, orbitals), orbitals)
-        qt_high[rows] = high
-        qt_low[rows] = low
+        qt_high[k] = high
+        qt_low[k] = low
 
     loads[0].wait()
     pre(0)
@@ -249,24 +252,32 @@
             q_copy(step, slot).wait_recv()
             transposed(2 * source + slot)
 
-    def product(rows, high, low):
-        dot = functools.partial(jnp.dot, preferred_element_type=jnp.float32)
-        first = qt_high[rows]
-        return dot(first, high) + (dot(first, low) + dot(qt_low[rows], high))
+    def stored_at(target):
+        found = jnp.int32(0)
+        for k in range(2 * nb):
+            found = jnp.where(slots[k] == target, jnp.int32(k), found)
+        return found
+
+    dot = functools.partial(jnp.dot, preferred_element_type=jnp.float32)
+
+    def product(buffer, phase, base, high, low):
+        for i in range(nb):
+            k = stored_at(base * nb + i)
+            first = qt_high[k]
+            buffer[phase, pl.ds(i * orbitals, orbitals)] = dot(first, high) + (
+                dot(first, low) + dot(qt_low[k], high)
+            )
 
     def part_copy(phase):
         return remote(
             part_out.at[phase], part_in.at[phase], part_send.at[phase], part_recv.at[phase], sub=other
         )
-
-    mine = pl.ds(pl.multiple_of(s * half, half), half)
-    theirs = pl.ds(pl.multiple_of(other * half, half), half)
 
     def start_gram(phase, field):
         high, low = split(field.reshape(cells_dev, orbitals))
-        part_out[phase] = product(theirs, high, low)
+        product(part_out, phase, other, high, low)
         part_copy(phase).start()
-        part_sum[phase] = product(mine, high, low)
+        product(part_sum, phase, s, high, low)
 
     def chunk_rows(c):
         return pl.ds(c * chunk, chunk)
@@ -330,10 +341,12 @@
             relay_down(phase)
             relay_up(phase)
 
+    outs = (corr, energy)
+
     def out_copy(phase, c):
         rows = pl.ds(pl.multiple_of(s * half + c * chunk, chunk), chunk)
         return remote(
-            out.at[phase, rows], out.at[phase, rows],
+            outs[phase].at[rows], outs[phase].at[rows],
             out_send.at[phase, c], out_recv.at[phase, c], sub=other,
         )
 
@@ -345,16 +358,16 @@
             @pl.when(g == 0)
             def _():
                 down_copy(phase, c, False).wait_recv()
-                out[phase, rows] = (own + from_high[phase, chunk_rows(c)]) * factor
+                outs[phase][rows] = (own + from_high[phase, chunk_rows(c)]) * factor
 
             @pl.when(g == nz - 1)
             def _():
                 up_copy(phase, c, False).wait_recv()
-                out[phase, rows] = (own + from_low[phase, chunk_rows(c)]) * factor
+                outs[phase][rows] = (own + from_low[phase, chunk_rows(c)]) * factor
 
             @pl.when(jnp.logical_and(g > 0, g < nz - 1))
             def _():
-                out[phase, rows] = (
+                outs[phase][rows] = (
                     to_high[phase, chunk_rows(c)] + from_high[phase, chunk_rows(c)]
                 ) * factor
 
@@ -417,27 +430,30 @@
     whole = pltpu.VMEM(cells, f32)
     gram = pltpu.VMEM((2, half, orbitals), f32)
     dma = pltpu.SemaphoreType.DMA
-    products = pl.pallas_call(
+    correlation, energy = pl.pallas_call(
         functools.partial(kernel, nz, nb),
-        out_shape=jax.ShapeDtypeStruct((2, stored * orbitals, orbitals), f32),
+        out_shape=(jax.ShapeDtypeStruct((stored * orbitals, orbitals), f32),) * 2,
         in_specs=[
-            pl.BlockSpec(memory_space=pl.ANY),
-            pl.BlockSpec(memory_space=pl.ANY),
-            pl.BlockSpec(memory_space=pltpu.VMEM),
-            pl.BlockSpec(memory_space=pltpu.VMEM),
+            pl.BlockSpec(memory_space=pltpu.SMEM),
+            pl.BlockSpec(memory_space=pltpu.HBM),
+            pl.BlockSpec(memory_space=pltpu.HBM),
+            pl.BlockSpec(memory_space=pltpu.HBM),
+            pl.BlockSpec(memory_space=pltpu.HBM),
         ],
-        out_specs=pl.BlockSpec(memory_space=pltpu.VMEM),
+        out_specs=(pl.BlockSpec(memory_space=pltpu.VMEM),) * 2,
         scratch_shapes=[
+            pltpu.VMEM(potential.shape, f32),
+            pltpu.VMEM((atom_plane.shape[0] // 128, 128), jnp.int32),
             padded, padded, padded, whole, whole, whole,
             pltpu.VMEM((3,) + cells, f32),
             pltpu.VMEM((stored,) + cells, f32),
-            pltpu.VMEM((stored * orbitals, cells_dev), jnp.bfloat16),
-            pltpu.VMEM((stored * orbitals, cells_dev), jnp.bfloat16),
+            pltpu.VMEM((stored, orbitals, cells_dev), jnp.bfloat16),
+            pltpu.VMEM((stored, orbitals, cells_dev), jnp.bfloat16),
             pltpu.VMEM((2, 8, orbitals), f32),
             pltpu.VMEM((ranks, width_x, orbitals), f32),
             pltpu.VMEM((ranks, width_x, orbitals), f32),
             gram, gram, gram, gram, gram, gram, gram,
-            dma((3,)),
+            dma((5,)),
             dma((3, 2)), dma((3, 2)), dma((3, 2)), dma((3, 2)),
             dma((nb, 2)), dma((nb, 2)),
             dma((ranks,)), dma((ranks,)), dma((ranks,)), dma((ranks,)),
@@ -446,23 +462,16 @@
             dma((2, CHUNKS)), dma((2, CHUNKS)),
         ],
         compiler_params=pltpu.CompilerParams(
-            collective_id=0, has_side_effects=True, vmem_limit_bytes=48 * 1024 * 1024
+            collective_id=0, has_side_effects=True, vmem_limit_bytes=60 * 1024 * 1024
         ),
         cost_estimate=pl.CostEstimate(
             flops=4 * cells_dev * orbitals * stored * orbitals,
             bytes_accessed=4 * orbitals * (3 * cells_dev + 2 * stored * orbitals),
             transcendentals=0,
         ),
-    )(filter_block, band_blocks, potential, atom_plane.reshape(-1, 128))
-    blocks = products.reshape(2, stored, orbitals, orbitals)
-    placed = []
-    for target in range(stored):
-        block = jnp.zeros((2, orbitals, orbitals), f32)
-        for k in range(stored):
-            block = jnp.where(block_slot[k] == target, blocks[:, k], block)
-        placed.append(block)
-    placed = jnp.stack(placed, axis=1)
-    return placed[0][None], placed[1][None]
+    )(block_slot, filter_block, band_blocks, potential, atom_plane.reshape(-1, 128))
+    shape = (1, stored, orbitals, orbitals)
+    return correlation.reshape(shape), energy.reshape(shape)
 
 
 def solution(mesh):

time: 59 us -> 48.1 us (0.82)
  between operations: 10.9 us -> 0.65 us
  local copies, waits for them, and re-layouts: 4.29 us -> 2.42 us
  Pallas kernels: 43.2 us -> 44.9 us
    slice x2 -> x0, local copies, waits for them, and re-layouts: 2.29 us -> none  [the longest x1 1.46 us: shards(): block = jnp.where(block_slot[k] == target, blocks[:, k], block)]
    pallas_call x1, Pallas kernels: 43.2 us -> 44.9 us  [shards(): pl.pallas_call(functools.partial(kernel, nz, nb), out_shape=(jax.ShapeDty...]
    unnamed x8 -> x4, local copies, waits for them, and re-layouts: 2 us -> 2.42 us
where the time goes in v2:
time: 48.1 us; the launch traced here: 47.9 us
  Pallas kernels  44.9 us (93%)
  local copies, waits for them, and re-layouts  2.42 us (5%)
  between operations  0.65 us (1%)
    pallas_call x1, Pallas kernels, shards(): pl.pallas_call(functools.partial(kernel, nz, nb), out_shape=(jax.ShapeDty...  44.9 us
    unnamed x4, local copies, waits for them, and re-layouts  2.42 us

profile of v2, /device:TPU:0, one launch (start us, length us, event | category | flops | bytes accessed | tf_op | source)
XLA Modules:
  0.0 47.9 jit_solution(7393332599340084123)
XLA Ops:
  0.6 44.9 %shard_map.68 = (f32[512,128]{1,0:T(8,128)}, f32[512,128]{1,0:T(8,128)}) custom-call(s32[4]{0:T(128)} %slots.1, f32[1,8,8,8,128]{4,3,2,1,0:T(8,128)} %x_hbm.1, f32[1,2,8,8,8,128]{5,4,3,2,1,0:T(8,128)} %q_hbm.1, f32[8,8,8]{2,1,0:T(8,128)} %pot_hbm.1, s32[16,128]{1,0:T(8,128)} %bitcast.5), custom_call_target="tpu_custom_call" | custom-call | flops 134217728 | bytes 1310720 | tf_op jit(solution)/shard_map/pallas_call | solution.py:433
  45.5 0.0 copy-start
  45.5 1.7 %copy.9 = f32[1,4,128,128]{3,2,1,0:T(8,128)} copy(f32[1,4,128,128]{3,2,1,0:T(8,128)} %bitcast.4) | data formatting | bytes 524288
  47.2 0.0 copy-done
  47.2 0.7 %copy.10 = f32[1,4,128,128]{3,2,1,0:T(8,128)} copy(f32[1,4,128,128]{3,2,1,0:T(8,128)S(1)} %bitcast.3) | data formatting | bytes 524288
Async XLA Ops:
  45.5 1.7 %copy-start = (f32[512,128]{1,0:T(8,128)S(1)}, f32[512,128]{1,0:T(8,128)}, u32[]{:S(2)}) copy-start(f32[512,128]{1,0:T(8,128)} %get-tuple-element.5) | copy-start | bytes 786436

commit v3 on v2

--- a/solution.py
+++ b/solution.py
@@ -34,7 +34,7 @@
 
 
 def kernel(
-    nz, nb, slots, x_hbm, q_hbm, pot_hbm, atoms_hbm, corr, energy,
+    nz, nb, slots, x_hbm, q_hbm, pot_hbm, atoms_hbm, out,
     pot, atoms, f0, f1, f2, applied, acc, eff, ypeer, qbuf, qt_high, qt_low,
     consts, tops, squares, part_out, part_in, part_sum, from_low, from_high, to_high, to_low,
     load_sem, z_send, z_recv, y_send, y_recv, q_send, q_recv,
@@ -341,12 +341,10 @@
             relay_down(phase)
             relay_up(phase)
 
-    outs = (corr, energy)
-
     def out_copy(phase, c):
         rows = pl.ds(pl.multiple_of(s * half + c * chunk, chunk), chunk)
         return remote(
-            outs[phase].at[rows], outs[phase].at[rows],
+            out.at[phase, rows], out.at[phase, rows],
             out_send.at[phase, c], out_recv.at[phase, c], sub=other,
         )
 
@@ -358,16 +356,16 @@
             @pl.when(g == 0)
             def _():
                 down_copy(phase, c, False).wait_recv()
-                outs[phase][rows] = (own + from_high[phase, chunk_rows(c)]) * factor
+                out[phase, rows] = (own + from_high[phase, chunk_rows(c)]) * factor
 
             @pl.when(g == nz - 1)
             def _():
                 up_copy(phase, c, False).wait_recv()
-                outs[phase][rows] = (own + from_low[phase, chunk_rows(c)]) * factor
+                out[phase, rows] = (own + from_low[phase, chunk_rows(c)]) * factor
 
             @pl.when(jnp.logical_and(g > 0, g < nz - 1))
             def _():
-                outs[phase][rows] = (
+                out[phase, rows] = (
                     to_high[phase, chunk_rows(c)] + from_high[phase, chunk_rows(c)]
                 ) * factor
 
@@ -376,14 +374,14 @@
     start_gram(0, f2[pl.ds(HALO, depth_z)])
     pre(2)
     reduce_sub(0)
+    wait_ranks(squares, square_send, square_recv)
+    total = jnp.sum(jnp.sum(squares[...], axis=0), axis=0, keepdims=True)
+    factor = lax.rsqrt(total / cells_all + EPSILON)
+    relay(0)
     finish_both(2)
     start_gram(1, applied[...])
-    relay(0)
+    conclude(0, factor)
     reduce_sub(1)
-    wait_ranks(squares, square_send, square_recv)
-    total = jnp.sum(jnp.sum(squares[...], axis=0), axis=0, keepdims=True)
-    factor = lax.rsqrt(total / cells_all + EPSILON) * (1.0 / math.sqrt(cells_all))
-    conclude(0, factor)
     relay(1)
     conclude(1, factor)
 
@@ -430,9 +428,9 @@
     whole = pltpu.VMEM(cells, f32)
     gram = pltpu.VMEM((2, half, orbitals), f32)
     dma = pltpu.SemaphoreType.DMA
-    correlation, energy = pl.pallas_call(
+    products = pl.pallas_call(
         functools.partial(kernel, nz, nb),
-        out_shape=(jax.ShapeDtypeStruct((stored * orbitals, orbitals), f32),) * 2,
+        out_shape=jax.ShapeDtypeStruct((2, stored * orbitals, orbitals), f32),
         in_specs=[
             pl.BlockSpec(memory_space=pltpu.SMEM),
             pl.BlockSpec(memory_space=pltpu.HBM),
@@ -440,7 +438,7 @@
             pl.BlockSpec(memory_space=pltpu.HBM),
             pl.BlockSpec(memory_space=pltpu.HBM),
         ],
-        out_specs=(pl.BlockSpec(memory_space=pltpu.VMEM),) * 2,
+        out_specs=pl.BlockSpec(memory_space=pltpu.VMEM),
         scratch_shapes=[
             pltpu.VMEM(potential.shape, f32),
             pltpu.VMEM((atom_plane.shape[0] // 128, 128), jnp.int32),
@@ -471,7 +469,8 @@
         ),
     )(block_slot, filter_block, band_blocks, potential, atom_plane.reshape(-1, 128))
     shape = (1, stored, orbitals, orbitals)
-    return correlation.reshape(shape), energy.reshape(shape)
+    norm_factor = 1.0 / math.sqrt(cells_dev * ranks)
+    return (products[0] * norm_factor).reshape(shape), (products[1] * norm_factor).reshape(shape)
 
 
 def solution(mesh):

time: 48.1 us -> 52.7 us (1.096)
  Pallas kernels: 44.9 us -> 50.1 us
  local copies, waits for them, and re-layouts: 2.42 us -> 0 us
  other arithmetic: 0 us -> 1.86 us
    pallas_call x1, Pallas kernels: 44.9 us -> 50.1 us  [shards(): pl.pallas_call(functools.partial(kernel, nz, nb), out_shape=jax.ShapeDtyp...]
    unnamed x4 -> x0, local copies, waits for them, and re-layouts: 2.42 us -> none
    mul x0 -> x1, other arithmetic: none -> 1.86 us  [shards(): products[1] * norm_factor]
where the time goes in v3:
time: 52.7 us; the launch traced here: 52.5 us
  Pallas kernels  50.1 us (95%)
  other arithmetic  1.86 us (4%)
  between operations  0.64 us (1%)
    pallas_call x1, Pallas kernels, shards(): pl.pallas_call(functools.partial(kernel, nz, nb), out_shape=jax.ShapeDtyp...  50.1 us
    mul x1, other arithmetic, shards(): products[1] * norm_factor  1.86 us

profile of v3, /device:TPU:0, one launch (start us, length us, event | category | flops | bytes accessed | tf_op | source)
XLA Modules:
  0.0 52.5 jit_solution(5282969996685119152)
XLA Ops:
  0.6 50.1 %shard_map.68 = f32[2,512,128]{2,1,0:T(8,128)} custom-call(s32[4]{0:T(128)} %slots.1, f32[1,8,8,8,128]{4,3,2,1,0:T(8,128)} %x_hbm.1, f32[1,2,8,8,8,128]{5,4,3,2,1,0:T(8,128)} %q_hbm.1, f32[8,8,8]{2,1,0:T(8,128)} %pot_hbm.1, s32[16,128]{1,0:T(8,128)} %bitcast.5), custom_call_target="tpu_custom_call" | custom-call | flops 134217728 | bytes 1310720 | tf_op jit(solution)/shard_map/pallas_call | solution.py:431
  50.7 1.9 %slice_multiply_fusion = (f32[1,512,128]{2,1,0:T(8,128)}, f32[1,512,128]{2,1,0:T(8,128)}) fusion(f32[2,512,128]{2,1,0:T(8,128)} %shard_map.68), kind=kLoop, calls=%fused_computation | loop fusion | flops 131072 | bytes 1048576 | tf_op jit(solution)/shard_map/mul | solution.py:473

commit v4 on v3

--- a/solution.py
+++ b/solution.py
@@ -377,12 +377,12 @@
     wait_ranks(squares, square_send, square_recv)
     total = jnp.sum(jnp.sum(squares[...], axis=0), axis=0, keepdims=True)
     factor = lax.rsqrt(total / cells_all + EPSILON)
-    relay(0)
     finish_both(2)
     start_gram(1, applied[...])
-    conclude(0, factor)
+    relay(0)
     reduce_sub(1)
     relay(1)
+    conclude(0, factor)
     conclude(1, factor)
 
     for phase in range(2):

time: 52.7 us -> 48.1 us (0.913)
  Pallas kernels: 50.1 us -> 45.5 us
    pallas_call x1, Pallas kernels: 50.1 us -> 45.5 us  [shards(): pl.pallas_call(functools.partial(kernel, nz, nb), out_shape=jax.ShapeDtyp...]
where the time goes in v4:
time: 48.1 us; the launch traced here: 47.9 us
  Pallas kernels  45.5 us (95%)
  other arithmetic  1.86 us (4%)
  between operations  0.64 us (1%)
    pallas_call x1, Pallas kernels, shards(): pl.pallas_call(functools.partial(kernel, nz, nb), out_shape=jax.ShapeDtyp...  45.5 us
    mul x1, other arithmetic, shards(): products[1] * norm_factor  1.86 us

profile of v4, /device:TPU:0, one launch (start us, length us, event | category | flops | bytes accessed | tf_op | source)
XLA Modules:
  0.0 47.9 jit_solution(995811650643233429)
XLA Ops:
  0.6 45.5 %shard_map.68 = f32[2,512,128]{2,1,0:T(8,128)} custom-call(s32[4]{0:T(128)} %slots.1, f32[1,8,8,8,128]{4,3,2,1,0:T(8,128)} %x_hbm.1, f32[1,2,8,8,8,128]{5,4,3,2,1,0:T(8,128)} %q_hbm.1, f32[8,8,8]{2,1,0:T(8,128)} %pot_hbm.1, s32[16,128]{1,0:T(8,128)} %bitcast.5), custom_call_target="tpu_custom_call" | custom-call | flops 134217728 | bytes 1310720 | tf_op jit(solution)/shard_map/pallas_call | solution.py:431
  46.1 1.9 %slice_multiply_fusion = (f32[1,512,128]{2,1,0:T(8,128)}, f32[1,512,128]{2,1,0:T(8,128)}) fusion(f32[2,512,128]{2,1,0:T(8,128)} %shard_map.68), kind=kLoop, calls=%fused_computation | loop fusion | flops 131072 | bytes 1048576 | tf_op jit(solution)/shard_map/mul | solution.py:473
